TPU v7x, 256 devices: a whole 4x4x8 slice. The times are simulated.
256 devices in a mesh: ctx: 16 (over z, y_lo), head: 8 (over y_hi, x), dp: 2 (over core).
Axes of the slice: x: 4, y: 4 (y_hi: 2, y_lo: 2; y = y_hi * 2 + y_lo), z: 8, core: 2. Of those that a mesh axis runs over, the one named last changes fastest.
Arguments:
- queries: bfloat16 [4096, 8192], P(('dp', 'ctx'), 'head'), parts along dimension 0, may hold values from -96 to 96
- keys_values: bfloat16 [2, 4096, 512], P(None, ('dp', 'ctx')), parts along dimension 1, may hold values from -4 to 4
- doc_lengths: int32 [16], P('dp'), parts along dimension 0, may hold values from 1 to 1024, 2048 in all
- residual: bfloat16 [4096, 4096], P(('dp', 'ctx', 'head')), parts along dimension 0, may hold values from -3 to 3
- out_weight: bfloat16 [8192, 4096], P('head', 'ctx'), may hold values from -0.25 to 0.25
- norm_gain: float32 [4096], replicated, may hold values from 0.1 to 1.9
- expert_ids: int32 [4096, 8], P(('dp', 'ctx', 'head')), parts along dimension 0, may hold values from 0 to 127, all different within a row; in each aligned block of 16 rows (0 to 15, 16 to 31, ...) at most 2 rows name the same one
- priority: int32 [4096], P(('dp', 'ctx', 'head')), parts along dimension 0, may hold values from 0 to 2047, each once
Outputs:
- hidden: bfloat16 [4096, 4096], P(('dp', 'ctx', 'head')), parts along dimension 0
- expert_rows: bfloat16 [128, 256, 2, 4096], P(('ctx', 'head'), 'dp'), parts along dimension 1
There are 2 independent parts, one for each index of `dp`. A program takes and returns all parts, laid end to end along the dimension named above; an argument that names none is the same for every part. Nothing has to cross between parts.
Inputs may be any that keep to these rules, and one draw needn't show every extreme that they name: `doc_lengths`: the documents lie end to end and fill the pack. `expert_ids`: each token names 8 different experts; the tokens of one block of 16 name one expert at most 2 times. `priority`: each position once.
All inputs are finite; a program needn't handle non-finite values.
Results may differ from a plain program's by a relative error of at most 0.017.
Values may be sent and summed in bfloat16 or wider, within the bound.
A program may use at most 64 MiB of HBM per device.

v0:
```python
import math

import jax
import jax.numpy as jnp
from jax import lax
from jax.sharding import PartitionSpec as P

HEADS = 64
KV_HEADS = 4
HEAD_DIM = 128
TOPK = 8


masked_low = -1e30


def doc_starts(positions, doc_lengths):
    ends = jnp.cumsum(doc_lengths)
    inside = ends[None, :] <= positions[:, None]
    return jnp.sum(jnp.where(inside, doc_lengths[None, :], 0), axis=1)


def block_update(
    current, query_block, positions, starts, key_block, value_block, key_first, key_width
):
    scale = 1.0 / math.sqrt(query_block.shape[-1])
    scores = (
        jnp.einsum("rkgd,ckd->kgrc", query_block, key_block, preferred_element_type=jnp.float32)
        * scale
    )
    key_positions = key_first + jnp.arange(key_width, dtype=jnp.int32)
    allowed = (key_positions[None, :] <= positions[:, None]) & (
        key_positions[None, :] >= starts[:, None]
    )
    running, totals, summed = current
    masked = jnp.where(allowed, scores, masked_low)
    highest = jnp.maximum(running, jnp.max(masked, axis=3))
    factor = jnp.exp(running - highest)
    weights = jnp.where(allowed, jnp.exp(masked - highest[..., None]), 0.0)
    totals = totals * factor + jnp.sum(weights, axis=3)
    summed = summed * factor[..., None] + jnp.einsum(
        "kgrc,ckd->kgrd",
        weights.astype(jnp.bfloat16),
        value_block,
        preferred_element_type=jnp.float32,
    )
    return (highest, totals, summed)


def attend(blocks, local_pairs, pair_heads, per_pair, head_dim):
    prepared = []
    initial = []
    for query_rows, positions, starts in blocks:
        query_count = query_rows.shape[0]
        shaped = query_rows.reshape(query_count, pair_heads, per_pair, head_dim)
        prepared.append((shaped, positions, starts, positions[-1], jnp.min(starts)))
        initial.append(
            (
                jnp.full((pair_heads, per_pair, query_count), masked_low, jnp.float32),
                jnp.zeros((pair_heads, per_pair, query_count), jnp.float32),
                jnp.zeros((pair_heads, per_pair, query_count, head_dim), jnp.float32),
            )
        )
    key_piece = lax.all_gather(local_pairs, "ctx", axis=1, tiled=True)
    row_count = key_piece.shape[1]
    key_width = 512
    block_count = row_count // key_width
    key_parts = key_piece[0].reshape(block_count, key_width, pair_heads, head_dim)
    value_parts = key_piece[1].reshape(block_count, key_width, pair_heads, head_dim)

    def step(states, inputs):
        key_block, value_block, block_number = inputs
        key_first = block_number * key_width
        updated = []
        for entry, current in zip(prepared, states):
            query_block, positions, starts, last_query, first_start = entry
            needed = (key_first <= last_query) & (key_first + key_width - 1 >= first_start)
            updated.append(
                lax.cond(
                    needed,
                    lambda present: block_update(
                        present,
                        query_block,
                        positions,
                        starts,
                        key_block,
                        value_block,
                        key_first,
                        key_width,
                    ),
                    lambda present: present,
                    current,
                )
            )
        return (tuple(updated), None)

    result, unused = lax.scan(
        step, tuple(initial), (key_parts, value_parts, jnp.arange(block_count, dtype=jnp.int32))
    )
    outputs = []
    for current in result:
        running, totals, summed = current
        mixed = summed / totals[..., None]
        query_count = mixed.shape[2]
        outputs.append(
            mixed.transpose(2, 0, 1, 3)
            .reshape(query_count, pair_heads * per_pair * head_dim)
            .astype(jnp.bfloat16)
        )
    return outputs


def local(queries, keys_values, doc_lengths, residual, out_weight, norm_gain, expert_ids, priority):
    ctx_count = lax.axis_size("ctx")
    head_count = lax.axis_size("head")
    ctx_index = lax.axis_index("ctx")
    head_index = lax.axis_index("head")
    local_tokens = queries.shape[0]
    head_dim = HEAD_DIM
    local_heads = queries.shape[1] // head_dim
    group_size = HEADS // KV_HEADS
    pair_heads = max(1, local_heads // group_size)
    per_pair = local_heads // pair_heads
    first_pair = head_index * local_heads // group_size
    local_pairs = lax.dynamic_slice_in_dim(
        keys_values, first_pair * head_dim, pair_heads * head_dim, 2
    )
    positions = ctx_index * local_tokens + jnp.arange(local_tokens, dtype=jnp.int32)
    results = attend(
        [(queries, positions, doc_starts(positions, doc_lengths))],
        local_pairs,
        pair_heads,
        per_pair,
        head_dim,
    )
    attended = results[0]
    model_width = residual.shape[1]
    row_count = residual.shape[0]
    partial_terms = jnp.dot(
        attended,
        lax.all_gather(out_weight, "ctx", axis=1, tiled=True),
        preferred_element_type=jnp.float32,
    )
    projected = lax.psum_scatter(
        partial_terms.astype(jnp.bfloat16), "head", scatter_dimension=0, tiled=True
    ).astype(jnp.float32)
    hidden = (residual.astype(jnp.float32) + projected).astype(jnp.bfloat16)
    hidden_wide = hidden.astype(jnp.float32)
    inverse = lax.rsqrt(jnp.mean(hidden_wide * hidden_wide, axis=1, keepdims=True) + 1e-06)
    normed = (hidden_wide * inverse * norm_gain[None, :]).astype(jnp.bfloat16)
    expert_count = ctx_count * head_count
    capacity = 2 * row_count * TOPK // expert_count
    expert_range = jnp.arange(expert_count, dtype=jnp.int32)
    chosen = jnp.sum(
        (expert_ids[:, :, None] == expert_range[None, None, :]).astype(jnp.int32), axis=1
    )
    earlier = (priority[:, None] < priority[None, :]).astype(jnp.int32)
    ranks = jnp.dot(earlier.T, chosen)
    slot_range = jnp.arange(capacity, dtype=jnp.int32)
    selection = (
        (chosen.T[:, None, :] == 1) & (ranks.T[:, None, :] == slot_range[None, :, None])
    ).astype(jnp.bfloat16)
    outgoing = jnp.einsum(
        "esr,rd->esd", selection, normed, preferred_element_type=jnp.float32
    ).astype(jnp.bfloat16)
    direct = outgoing.reshape(expert_count, 1, capacity, model_width)
    expert_rows = lax.all_to_all(direct, ("ctx", "head"), split_axis=0, concat_axis=1, tiled=True)
    return (hidden, expert_rows)


def solution(mesh):
    return jax.shard_map(
        local,
        mesh=mesh,
        in_specs=(
            P(("dp", "ctx"), "head"),
            P(None, ("dp", "ctx"), None),
            P("dp"),
            P(("dp", "ctx", "head"), None),
            P("head", "ctx"),
            P(),
            P(("dp", "ctx", "head"), None),
            P(("dp", "ctx", "head")),
        ),
        out_specs=(P(("dp", "ctx", "head"), None), P(("ctx", "head"), "dp", None, None)),
        check_vma=False,
    )
```

profile of v0, /device:TPU:2, one launch (start us, length us, event | category | flops | bytes accessed | tf_op | source)
XLA Modules:
  0.0 438.3 jit_solution(17654980720588801359)
XLA Ops:
  7.2 0.9 copy-done
  8.1 0.6 constant_dynamic-slice_fusion
  8.8 0.7 all-gather.5.cloned.1.call-update
  9.6 0.8 reduce-window.8
  10.4 0.7 slice.9
  11.1 1.1 copy.26
  12.4 0.7 select_reduce_fusion
  13.1 0.7 reduce_min.9
  13.8 68.2 %all-gather.3.cloned.1.call-done = bf16[2,2048,128]{2,1,0:T(8,128)(2,1)} async-done(((bf16[2,128,128]{2,1,0:T(8,128)(2,1)}), bf16[2,2048,128]{2,1,0:T(8,128)(2,1)}) %all-gather.3.cloned.1.call-update) | async-done | bytes 1048592 | tf_op jit(solution)/shard_map/all_gather | solution.py:64
  82.0 1.3 fusion.41
  83.4 12.5 %while.19 = (s32[]{:T(128)}, f32[1,8,128]{2,1,0:T(8,128)S(1)}, f32[1,8,128]{2,1,0:T(8,128)S(1)}, f32[1,8,128,128]{3,2,1,0:T(8,128)S(1)}, s32[4]{0:T(128)S(1)}, /...) while((s32[]{:T(128)}, f32[1,8,128]{2,1,0:T(8,128)S(1)}, ...), condition=%wide.region_8.9_spmd.clone, body=%wide.region_3.8_spmd.clone.sunk | while | flops 275713664 | bytes 8199019 | solution.py:97
  83.4 0.6 dynamic_slice.46
  85.9 2.1 conditional.3
  87.1 0.8 fusion.5
  88.0 0.6 dynamic_slice.46
  93.2 0.6 dynamic_slice.46
  96.1 187.3 %all-gather.5.cloned.1.call-done = bf16[1024,4096]{1,0:T(8,128)(2,1)} async-done(((bf16[1024,256]{1,0:T(8,128)(2,1)}), bf16[1024,4096]{1,0:T(8,128)(2,1)}) %all-gather.5.cloned.1.call-update) | async-done | bytes 8388624 | tf_op jit(solution)/shard_map/all_gather | solution.py:141
  283.4 5.7 %convolution_convert_fusion.1 = bf16[128,4096]{1,0:T(8,128)(2,1)} fusion(bf16[128,1024]{0,1:T(8,128)(2,1)S(1)} %bitcast.73, bf16[1024,4096]{1,0:T(8,128)(2,1)} %all-gather.5.cloned.1.call-done), kind=kOutput, calls=%fused_computation.34 | convolution fusion | flops 1074266112 | bytes 9699328 | tf_op jit(solution)/shard_map/dot_general | solution.py:139
  289.6 74.3 %reduce-scatter.2.cloned.1.call-done = bf16[16,4096]{1,0:T(8,128)(2,1)} async-done(((bf16[128,4096]{1,0:T(8,128)(2,1)}), bf16[16,4096]{1,0:T(8,128)(2,1)}) %reduce-scatter.2.cloned.1.call-update) | async-done | bytes 131088 | tf_op jit(solution)/shard_map/reduce_scatter | solution.py:144
  363.9 1.1 fusion.26
  365.0 0.8 fusion.25
  365.8 2.2 copy.30
  368.0 62.5 %all_to_all.12 = bf16[128,1,2,4096]{3,2,1,0:T(2,128)(2,1)S(1)} all-to-all(bf16[128,1,2,4096]{3,2,1,0:T(2,128)(2,1)S(1)} %copy.30), channel_id=1, replica_groups=mesh['ctx'=16,'head'=8,'dp'=2] {'ctx','head'}, dimensions={0} | all-to-all | bytes 4194304 | tf_op jit(solution)/shard_map/all_to_all | solution.py:167
  430.5 1.3 copy.53
  (45 shorter events, 2.9 us)
Async XLA Ops:
  7.2 1.0 copy-start
  7.2 74.8 %all-gather.3.cloned.1.call-start = ((), (), s32[]{:S(2)}) async-start(), calls=%async_computation.2 | async-start | bytes 1114112 | tf_op jit(solution)/shard_map/all_gather | solution.py:64
  8.8 274.6 %all-gather.5.cloned.1.call-start = ((), (), s32[]{:S(2)}) async-start(), calls=%async_computation.3 | async-start | bytes 8912896 | tf_op jit(solution)/shard_map/all_gather | solution.py:141
  9.5 354.4 %reduce-scatter.2.cloned.1.call-start = ((), (), s32[]{:S(2)}) async-start(), calls=%async_computation.4 | async-start | bytes 1179648 | tf_op jit(solution)/shard_map/reduce_scatter | solution.py:144
  283.4 5.7 %copy-start.4 = (s32[16,8]{0,1:T(8,128)S(1)}, s32[16,8]{0,1:T(8,128)}, u32[]{:S(2)}) copy-start(s32[16,8]{0,1:T(8,128)} %param.18) | copy-start | bytes 1540
  283.4 5.9 %copy-start.5 = (s32[16]{0:T(128)S(1)}, s32[16]{0:T(128)}, u32[]{:S(2)}) copy-start(s32[16]{0:T(128)} %param.19) | copy-start | bytes 196
  283.4 80.5 %copy-start.2 = (bf16[16,4096]{1,0:T(8,128)(2,1)S(1)}, bf16[16,4096]{1,0:T(8,128)(2,1)}, u32[]{:S(2)}) copy-start(bf16[16,4096]{1,0:T(8,128)(2,1)} %param.15) | copy-start | bytes 393220
  283.4 81.6 %copy-start.3 = (f32[4096]{0:T(1024)S(1)}, f32[4096]{0:T(1024)}, u32[]{:S(2)}) copy-start(f32[4096]{0:T(1024)} %param.17) | copy-start | bytes 49156
  365.0 3.0 copy-start.1
Sparse Core Ops, SparseCore 0:
  10.4 71.5 all-gather.2
  83.7 199.6 all-gather.4
  289.3 74.6 reduce-scatter.1
where the time goes:
time: 439 us; the launch traced here: 438 us
  waiting for transfers between devices  331 us (75%)
  blocking collectives  62.5 us (14%)
  between operations  13.9 us (3%)
  local copies, waits for them, and re-layouts  10.9 us (2%)
  loops' own time  8.12 us (2%)
  matrix products  7.99 us (2%)
    all_gather x1, waiting for transfers between devices, local(): lax.all_gather(out_weight, 'ctx', axis=1, tiled=True)  187 us
    reduce_scatter x1, waiting for transfers between devices, local(): lax.psum_scatter(partial_terms.astype(jnp.bfloat16), 'head', scatter_dime...  74.3 us
    all_gather x1, waiting for transfers between devices, attend(): key_piece = lax.all_gather(local_pairs, 'ctx', axis=1, tiled=True)  68.2 us
    all_to_all x1, blocking collectives, local(): lax.all_to_all(direct, ('ctx', 'head'), split_axis=0, concat_axis=1, tile...  62.5 us
  transfers between devices with their start and end apart: 3, of which 3 were waited for; matrix products, arithmetic and copies ran while one was open for 2% of the time, Pallas kernels for 0%

commit v1 on v0

v1 whole, which is shorter than its diff:
```python
import math

import jax
import jax.numpy as jnp
from jax import lax
from jax.experimental import pallas as pl
from jax.experimental.pallas import tpu as pltpu
from jax.sharding import PartitionSpec as P

D = 4096
HEAD_DIM = 128
HEADS_DEV = 8
ROWS = 128
KV_GROUP = 2
DOCS = 8
TOPK = 8
NZ = 8
PLANE = 16
REACH = 5
CHUNKS = 4
CW = D // CHUNKS
LOW = -1e30
COEF = math.log2(math.e) / math.sqrt(HEAD_DIM)
MESH = pl.DeviceIdType.MESH
OFFSET = (0, -1, -2, -3, 1, 2, 3, 4)
ORDER = (0, 1, 4, 2, 5, 3, 6, 7)


def kernel(
    q_ref, kv_ref, doc_ref, res_ref, w_ref, gain_ref, ids_ref, prio_ref,
    hid_ref, rows_ref,
    qbuf, kvbuf, vext, bias, mx, acc, att, wbuf, mt, mtbuf, sel, psend, prec, xbuf, asend,
    kvu_s, kvu_r, kvy_s, kvy_r, q_s, q_r, w_s, w_r, ws_s, ws_r, mt_s, mt_r,
    p_s, p_r, x_s, x_r, a_s, a_r, l_s,
):
    ctx = lax.axis_index("ctx")
    head = lax.axis_index("head")
    core = lax.axis_index("dp")
    z = ctx // 2
    ylo = ctx % 2
    me = ylo * 8 + head

    def at_z(k):
        return {"ctx": ((z + k + NZ) % NZ) * 2 + ylo}

    def at_plane(p):
        return {"ctx": z * 2 + p // 8, "head": p % 8}

    partner = {"ctx": z * 2 + (1 - ylo)}
    sibling = {"dp": 1 - core}

    def remote(src, dst, s, r, to):
        return pltpu.make_async_remote_copy(
            src_ref=src, dst_ref=dst, send_sem=s, recv_sem=r, device_id=to, device_id_type=MESH
        )

    def wait_for(ref, sem):
        pltpu.make_async_copy(ref, ref, sem).wait()

    barrier = pltpu.get_barrier_semaphore()

    def greet_plane(j, c):
        pl.semaphore_signal(barrier, inc=1, device_id=at_plane((me + j) % PLANE), device_id_type=MESH)
        return c

    def greet_z(j, c):
        pl.semaphore_signal(barrier, inc=1, device_id=at_z(j), device_id_type=MESH)
        return c

    lax.fori_loop(1, PLANE, greet_plane, 0)
    lax.fori_loop(1, NZ, greet_z, 0)
    pl.semaphore_signal(barrier, inc=1, device_id=sibling, device_id_type=MESH)

    key_head = pl.multiple_of((head // KV_GROUP) * HEAD_DIM, HEAD_DIM)
    for i in range(2):
        kvbuf[0, i, ylo] = kv_ref[i, :, pl.ds(key_head, HEAD_DIM)]
    qbuf[ylo] = q_ref[...]

    row16 = lax.broadcasted_iota(jnp.int32, (16, 128), 0)
    lane16 = lax.broadcasted_iota(jnp.int32, (16, 128), 1)
    chosen = jnp.zeros((16, 128), jnp.float32)
    for k in range(TOPK):
        chosen = chosen + jnp.where(ids_ref[:, k : k + 1] == lane16, 1.0, 0.0)
    prio_row = jnp.full((16, 128), 1 << 20, jnp.int32)
    prio_col = jnp.zeros((16, 128), jnp.int32)
    for u in range(16):
        prio_row = jnp.where(lane16 == u, prio_ref[u], prio_row)
        prio_col = jnp.where(row16 == u, prio_ref[u], prio_col)
    earlier = jnp.where((prio_row < prio_col) & (lane16 < 16), 1.0, 0.0)[:, :16]
    ranks = jnp.dot(
        earlier.astype(jnp.bfloat16), chosen.astype(jnp.bfloat16), preferred_element_type=jnp.float32
    )
    slots = jnp.where(chosen > 0.5, ranks + 1.0, 0.0)
    place = jnp.where(lane16 == row16 + 16 * z, 1.0, 0.0)
    mt[...] = lax.dot_general(
        slots.astype(jnp.bfloat16),
        place.astype(jnp.bfloat16),
        (((0,), (0,)), ((), ())),
        preferred_element_type=jnp.float32,
    )

    pl.semaphore_wait(barrier, PLANE - 1 + NZ - 1 + 1)

    half = pl.ds(pl.multiple_of(core * 512, 512), 512)

    def kv_up(r):
        return remote(kvbuf.at[r - 1, :, ylo], kvbuf.at[r, :, ylo], kvu_s.at[r], kvu_r.at[r], at_z(1))

    def kv_side(r):
        return remote(kvbuf.at[r, :, ylo], kvbuf.at[r, :, ylo], kvy_s.at[r], kvy_r.at[r], partner)

    def w_ring(s):
        first = s in (1, 4)
        src = w_ref.at[half, :] if first else wbuf.at[s - 1, half, :]
        return remote(src, wbuf.at[s, half, :], w_s.at[s], w_r.at[s], at_z(1 if s < 4 else -1))

    def w_side(s):
        return remote(wbuf.at[s, half, :], wbuf.at[s, half, :], ws_s.at[s], ws_r.at[s], sibling)

    q_swap = remote(qbuf.at[ylo], qbuf.at[ylo], q_s, q_r, partner)
    kv_up(1).start()
    kv_side(0).start()
    w_ring(4).start()
    w_ring(1).start()
    q_swap.start()

    def mt_copy(j):
        to = (z + j) % NZ
        rows = pl.ds(pl.multiple_of(to * 16, 16), 16)
        return remote(mt.at[rows, :], mtbuf.at[z], mt_s, mt_r, at_z(j))

    def mt_send(j, c):
        mt_copy(j).start()
        return c

    lax.fori_loop(1, NZ, mt_send, 0)
    mtbuf[z] = mt[pl.ds(pl.multiple_of(z * 16, 16), 16), :]

    def w_forward(s):
        remote_in = w_ring(s)
        remote_in.wait_recv()
        if s not in (3, 7):
            w_ring(s + 1).start()
        w_side(s).start()

    vext[:, HEAD_DIM:] = jnp.ones((2 * ROWS, HEAD_DIM), jnp.bfloat16)
    row = lax.broadcasted_iota(jnp.int32, (ROWS, 2 * ROWS), 0)
    lane = lax.broadcasted_iota(jnp.int32, (ROWS, 2 * ROWS), 1)

    def attend(r, yq):
        key_pos = ((z - r + NZ) % NZ) * 256 + lane
        pos = (2 * z + yq) * ROWS + row
        start = jnp.zeros((ROWS, 2 * ROWS), jnp.int32)
        end = jnp.int32(0)
        for d in range(DOCS):
            length = doc_ref[d]
            end = end + length
            start = start + jnp.where(pos >= end, length, 0)
        bias[...] = jnp.where((key_pos <= pos) & (key_pos >= start), 0.0, LOW)
        vext[:, :HEAD_DIM] = kvbuf[r, 1].reshape(2 * ROWS, HEAD_DIM)

        def one(h, c):
            b = yq * HEADS_DEV + h
            cols = pl.ds(pl.multiple_of(h * HEAD_DIM, HEAD_DIM), HEAD_DIM)
            s = lax.dot_general(
                qbuf[yq, :, cols],
                kvbuf[r, 0].reshape(2 * ROWS, HEAD_DIM),
                (((1,), (1,)), ((), ())),
                preferred_element_type=jnp.float32,
            )
            s = s + bias[...]
            top = jnp.max(s, axis=1, keepdims=True)
            if r > 0:
                old = mx[b]
                new = jnp.maximum(old, top)
            else:
                new = jnp.broadcast_to(top, (ROWS, HEAD_DIM))
            wide = jnp.concatenate([new, new], axis=1)
            weight = jnp.exp2((s - wide) * COEF).astype(jnp.bfloat16)
            out = jnp.dot(weight, vext[...], preferred_element_type=jnp.float32)
            if r > 0:
                factor = jnp.exp2((old - new) * COEF)
                out = out + acc[b] * jnp.concatenate([factor, factor], axis=1)
            if r < REACH - 1:
                mx[b] = new
                acc[b] = out
            else:
                rows = pl.ds(pl.multiple_of(yq * ROWS, ROWS), ROWS)
                att[rows, cols] = (out[:, :HEAD_DIM] / out[:, HEAD_DIM:]).astype(jnp.bfloat16)
            return c

        lax.fori_loop(0, HEADS_DEV, one, 0)

    def kv_step(r):
        kv_up(r).wait_recv()
        if r < REACH - 1:
            kv_up(r + 1).start()
        kv_side(r).start()
        kv_side(r).wait_recv()

    kv_side(0).wait_recv()
    attend(0, ylo)
    kv_step(1)
    attend(1, ylo)
    kv_step(2)
    attend(2, ylo)
    w_forward(4)
    w_forward(1)
    kv_step(3)
    attend(3, ylo)
    q_swap.wait_recv()
    attend(0, 1 - ylo)
    attend(1, 1 - ylo)
    attend(2, 1 - ylo)
    w_forward(5)
    w_forward(2)
    attend(3, 1 - ylo)
    kv_step(4)
    attend(4, ylo)
    attend(4, 1 - ylo)

    def p_copy(o, j):
        to = (me + j) % PLANE
        rows = pl.ds(pl.multiple_of(to * 16, 16), 16)
        return remote(psend.at[o, rows, :], prec.at[o, me], p_s.at[o], p_r.at[o], at_plane(to))

    def project(o):
        if o == 0:
            part = jnp.dot(att[...], w_ref[...], preferred_element_type=jnp.float32)
        else:
            w_side(o).wait_recv()
            part = jnp.dot(att[...], wbuf[o], preferred_element_type=jnp.float32)
        psend[o] = part.astype(jnp.bfloat16)
        prec[o, me] = psend[o, pl.ds(pl.multiple_of(me * 16, 16), 16), :]

        def send(j, c):
            p_copy(o, j).start()
            return c

        lax.fori_loop(1, PLANE, send, 0)

    project(0)
    project(4)
    project(1)
    w_forward(6)
    w_forward(3)
    project(5)
    project(2)
    w_forward(7)
    project(6)
    project(3)
    project(7)

    wait_for(mtbuf.at[pl.ds(0, NZ - 1)], mt_r)
    table = mtbuf[0]
    for i in range(1, NZ):
        table = table + mtbuf[i]
    want = jnp.where(lane16 // 16 == row16 // 2, (row16 % 2 + 1).astype(jnp.float32), -1.0)
    for d in range(PLANE):
        hit = jnp.broadcast_to(table[d : d + 1, :], (16, 128)) == want
        sel[pl.ds(d * 16, 16), :] = jnp.where(hit, 1.0, 0.0).astype(jnp.bfloat16)

    squares = jnp.zeros((16, 1), jnp.float32)
    for o in ORDER:
        wait_for(prec.at[o, pl.ds(0, PLANE - 1)], p_r.at[o])
        for side in range(2):
            total = jnp.zeros((16, 256), jnp.float32)
            for h in range(8):
                total = total + prec[o, side * 8 + h].astype(jnp.float32)
            first = ((z + OFFSET[o] + NZ) % NZ) * 2 + side
            cols = pl.ds(pl.multiple_of(first * 256, 256), 256)
            hidden = (res_ref[:, cols].astype(jnp.float32) + total).astype(jnp.bfloat16)
            hid_ref[:, cols] = hidden
            wide = hidden.astype(jnp.float32)
            squares = squares + jnp.sum(wide * wide, axis=1, keepdims=True)
    inverse = lax.rsqrt(squares / D + 1e-06)

    def x_copy(g, j):
        cols = pl.ds(g * CW, CW)
        return remote(xbuf.at[z, :, cols], xbuf.at[z, :, cols], x_s.at[g], x_r.at[g], at_z(j))

    for g in range(CHUNKS):
        cols = slice(g * CW, (g + 1) * CW)
        normed = hid_ref[:, cols].astype(jnp.float32) * inverse * gain_ref[:, cols]
        xbuf[z, :, cols] = normed.astype(jnp.bfloat16)

        def send_x(j, c, g=g):
            x_copy(g, j).start()
            return c

        lax.fori_loop(1, NZ, send_x, 0)

    def a_copy(g, j):
        to = (me + j) % PLANE
        cols = pl.ds(g * CW, CW)
        return remote(asend.at[to, :, cols], rows_ref.at[me, :, cols], a_s.at[g], a_r.at[g], at_plane(to))

    def own_copy(g):
        cols = pl.ds(g * CW, CW)
        return pltpu.make_async_copy(asend.at[me, :, cols], rows_ref.at[me, :, cols], l_s.at[g])

    for g in range(CHUNKS):
        cols = slice(g * CW, (g + 1) * CW)
        wait_for(xbuf.at[pl.ds(0, NZ - 1), :, pl.ds(g * CW, CW)], x_r.at[g])
        gathered = xbuf[:, :, cols].reshape(ROWS, CW)
        picked = jnp.dot(sel[...], gathered, preferred_element_type=jnp.float32)
        asend[:, :, cols] = picked.astype(jnp.bfloat16).reshape(PLANE, 16, CW)

        def send_a(j, c, g=g):
            a_copy(g, j).start()
            return c

        lax.fori_loop(1, PLANE, send_a, 0)
        own_copy(g).start()

    for r in range(1, REACH):
        kv_up(r).wait_send()
    for r in range(REACH):
        kv_side(r).wait_send()
    q_swap.wait_send()
    for s in range(1, NZ):
        w_ring(s).wait_send()
        w_side(s).wait_send()
    wait_for(mtbuf.at[pl.ds(0, NZ - 1)], mt_s)
    for o in range(NZ):
        wait_for(prec.at[o, pl.ds(0, PLANE - 1)], p_s.at[o])
    for g in range(CHUNKS):
        wait_for(xbuf.at[pl.ds(0, NZ - 1), :, pl.ds(g * CW, CW)], x_s.at[g])
        wait_for(asend.at[pl.ds(0, PLANE - 1), :, pl.ds(g * CW, CW)], a_s.at[g])
        own_copy(g).wait()
    for g in range(CHUNKS):
        wait_for(asend.at[pl.ds(0, PLANE - 1), :, pl.ds(g * CW, CW)], a_r.at[g])


def local(queries, keys_values, doc_lengths, residual, out_weight, norm_gain, expert_ids, priority):
    vmem = pl.BlockSpec(memory_space=pltpu.VMEM)
    smem = pl.BlockSpec(memory_space=pltpu.SMEM)
    bf16, f32 = jnp.bfloat16, jnp.float32
    dma = pltpu.SemaphoreType.DMA
    hidden, rows = pl.pallas_call(
        kernel,
        out_shape=(
            jax.ShapeDtypeStruct((16, D), bf16),
            jax.ShapeDtypeStruct((PLANE, 16, D), bf16),
        ),
        in_specs=[vmem, vmem, smem, vmem, vmem, vmem, vmem, smem],
        out_specs=(vmem, pl.BlockSpec(memory_space=pl.ANY)),
        scratch_shapes=[
            pltpu.VMEM((2, ROWS, 1024), bf16),
            pltpu.VMEM((REACH, 2, 2, ROWS, HEAD_DIM), bf16),
            pltpu.VMEM((2 * ROWS, 2 * HEAD_DIM), bf16),
            pltpu.VMEM((ROWS, 2 * ROWS), f32),
            pltpu.VMEM((16, ROWS, HEAD_DIM), f32),
            pltpu.VMEM((16, ROWS, 2 * HEAD_DIM), f32),
            pltpu.VMEM((2 * ROWS, 1024), bf16),
            pltpu.VMEM((NZ, 1024, 256), bf16),
            pltpu.VMEM((128, 128), f32),
            pltpu.VMEM((NZ, 16, 128), f32),
            pltpu.VMEM((256, 128), bf16),
            pltpu.VMEM((NZ, 256, 256), bf16),
            pltpu.VMEM((NZ, PLANE, 16, 256), bf16),
            pltpu.VMEM((NZ, 16, D), bf16),
            pltpu.VMEM((PLANE, 16, D), bf16),
            dma((REACH,)), dma((REACH,)), dma((REACH,)), dma((REACH,)),
            dma(()), dma(()),
            dma((NZ,)), dma((NZ,)), dma((NZ,)), dma((NZ,)),
            dma(()), dma(()),
            dma((NZ,)), dma((NZ,)),
            dma((CHUNKS,)), dma((CHUNKS,)), dma((CHUNKS,)), dma((CHUNKS,)), dma((CHUNKS,)),
        ],
        compiler_params=pltpu.CompilerParams(
            collective_id=0, has_side_effects=True, vmem_limit_bytes=48 * 1024 * 1024
        ),
    )(
        queries, keys_values, doc_lengths, residual, out_weight,
        norm_gain.reshape(1, D), expert_ids, priority,
    )
    rows = rows.reshape(PLANE, NZ, 2, D).transpose(1, 0, 2, 3).reshape(1, PLANE * NZ, 2, D)
    return hidden, rows


def solution(mesh):
    return jax.shard_map(
        local,
        mesh=mesh,
        in_specs=(
            P(("dp", "ctx"), "head"),
            P(None, ("dp", "ctx"), None),
            P("dp"),
            P(("dp", "ctx", "head"), None),
            P("head", "ctx"),
            P(),
            P(("dp", "ctx", "head"), None),
            P(("dp", "ctx", "head")),
        ),
        out_specs=(P(("dp", "ctx", "head"), None), P(("ctx", "head"), "dp", None, None)),
        check_vma=False,
    )
```

time: 439 us -> 126 us (0.29)
  waiting for transfers between devices: 331 us -> 0 us
  Pallas kernels: 0 us -> 109 us
  blocking collectives: 62.5 us -> 0 us
  between operations: 13.9 us -> 0.65 us
  loops' own time: 8.12 us -> 0 us
  matrix products: 7.99 us -> 0 us
  local copies, waits for them, and re-layouts: 10.9 us -> 15.5 us
    all_gather x2 -> x0, waiting for transfers between devices: 256 us -> none  [the longest x1 187 us: local(): lax.all_gather(out_weight, 'ctx', axis=1, tiled=True)]
    pallas_call x0 -> x1, Pallas kernels: none -> 109 us  [local(): pl.pallas_call(kernel, out_shape=(jax.ShapeDtypeStruct((16, D), bf16), ja...]
    reduce_scatter x1 -> x0, waiting for transfers between devices: 74.3 us -> none  [local(): lax.psum_scatter(partial_terms.astype(jnp.bfloat16), 'head', scatter_dime...]
    all_to_all x1 -> x0, blocking collectives: 62.5 us -> none  [local(): lax.all_to_all(direct, ('ctx', 'head'), split_axis=0, concat_axis=1, tile...]
    another operation x5 -> x0, loops' own time: 8.12 us -> none  [the longest x1 8 us: attend(): lax.scan(step, tuple(initial), (key_parts, value_parts, jnp.arange(block_...]
    dot_general x5 -> x0, matrix products: 7.99 us -> none  [the longest x1 5.67 us: local(): jnp.dot(attended, lax.all_gather(out_weight, 'ctx', axis=1, tiled=True),...]
    transpose x0 -> x1, local copies, waits for them, and re-layouts: none -> 5.6 us  [local(): rows.reshape(PLANE, NZ, 2, D).transpose(1, 0, 2, 3)]
  transfers between devices with their start and end apart: 3 -> 0, of which waited for: 3 -> 0; matrix products, arithmetic and copies ran while one was open for 2% -> 0% of each run, Pallas kernels for 0% -> 0%
where the time goes in v1:
time: 126 us; the launch traced here: 125 us
  Pallas kernels  109 us (87%)
  local copies, waits for them, and re-layouts  15.5 us (12%)
    pallas_call x1, Pallas kernels, local(): pl.pallas_call(kernel, out_shape=(jax.ShapeDtypeStruct((16, D), bf16), ja...  109 us
    unnamed x16, local copies, waits for them, and re-layouts  7.28 us
    transpose x1, local copies, waits for them, and re-layouts, local(): rows.reshape(PLANE, NZ, 2, D).transpose(1, 0, 2, 3)  5.6 us
    reshape x1, local copies, waits for them, and re-layouts, local(): rows.reshape(PLANE, NZ, 2, D).transpose(1, 0, 2, 3)  2.63 us

profile of v1, /device:TPU:2, one launch (start us, length us, event | category | flops | bytes accessed | tf_op | source)
XLA Modules:
  0.0 124.9 jit_solution(13275323532736042061)
XLA Ops:
  0.6 0.8 copy.10.ids_ref
  1.4 0.0 copy-start
  1.4 1.0 copy-done
  2.4 0.0 copy-start.1
  2.4 0.9 copy-done.1
  3.4 0.0 copy-start.2
  3.4 0.9 copy-done.2
  4.3 0.0 copy-start.3
  4.3 0.9 copy-done.3
  5.2 0.0 copy-start.4
  5.2 0.7 copy-done.4
  6.0 0.0 copy-start.5
  6.0 0.7 copy-done.5
  6.6 0.0 copy-start.6
  6.6 0.7 copy-done.6
  7.3 108.7 %shard_map.95 = (bf16[16,4096]{1,0:T(8,128)(2,1)S(1)}, bf16[16,16,4096]{2,1,0:T(8,128)(2,1)S(1)}) custom-call(bf16[128,1024]{1,0:T(8,128)(2,1)S(1)} %copy-done.1, bf16[2,128,512]{2,1,0:T(8,128)(2,1)S(1)} %copy-done.2, s32[8]{0:T(128)S(1)} %copy-done.5, bf16[16,4096]{1,0:T(8,128)(2,1)S(1)} %copy-done.3, bf16[1024,256]{1,0:T(8,128)(2,1)S(1)} %copy-done, ...), custom_call_target="tpu_custom_call" | custom-call | tf_op jit(solution)/shard_map/pallas_call | solution.py:340
  116.0 2.6 %reshape.14 = bf16[16,8,2,4096]{3,2,1,0:T(2,128)(2,1)} reshape(bf16[16,16,4096]{2,1,0:T(8,128)(2,1)S(1)} %get-tuple-element.5) | data formatting | bytes 4194304 | tf_op jit(solution)/shard_map/reshape | solution.py:378
  118.6 5.6 %copy.11 = bf16[8,16,2,4096]{3,2,1,0:T(2,128)(2,1)} copy(bf16[8,16,2,4096]{3,2,0,1:T(2,128)(2,1)} %bitcast.4) | data formatting | bytes 4194304 | tf_op jit(solution)/shard_map/transpose | solution.py:378
  124.2 0.7 copy.13
Async XLA Ops:
  1.4 1.0 copy-start
  2.4 0.9 copy-start.1
  3.4 0.9 copy-start.2
  4.3 0.9 copy-start.3
  5.2 0.7 copy-start.4
  6.0 0.7 copy-start.5
  6.6 0.7 copy-start.6

commit v2 on v1

v2 whole, which is shorter than its diff:
```python
import math

import jax
import jax.numpy as jnp
from jax import lax
from jax.experimental import pallas as pl
from jax.experimental.pallas import tpu as pltpu
from jax.sharding import PartitionSpec as P

D = 4096
HEAD_DIM = 128
HEADS_DEV = 8
ROWS = 128
KV_GROUP = 2
DOCS = 8
TOPK = 8
NZ = 8
PLANE = 16
REACH = 5
CHUNKS = 4
CW = D // CHUNKS
WCH = 2
WROWS = 512 // WCH
LOW = -1e30
COEF = math.log2(math.e) / math.sqrt(HEAD_DIM)
MESH = pl.DeviceIdType.MESH
OFFSET = (0, -1, -2, -3, 1, 2, 3, 4)
ORDER = (0, 1, 4, 2, 5, 3, 6, 7)


def kernel(
    q_ref, kv_ref, doc_ref, res_ref, w_ref, gain_ref, ids_ref, prio_ref,
    hid_ref, rows_ref,
    qbuf, kvbuf, vt, mx, acc, att, wbuf, res, gain, ids, prio, docs, mt, mtbuf, sel, psend, prec,
    xbuf, asend,
    in_s, kvu_s, kvu_r, kvy_s, kvy_r, q_s, q_r, w_s, w_r, ws_s, ws_r, mt_s, mt_r,
    p_s, p_r, x_s, x_r, a_s, a_r, l_s,
):
    ctx = lax.axis_index("ctx")
    head = lax.axis_index("head")
    core = lax.axis_index("dp")
    z = ctx // 2
    ylo = ctx % 2
    me = ylo * 8 + head

    def at_z(k):
        return {"ctx": ((z + k + NZ) % NZ) * 2 + ylo}

    def at_plane(p):
        return {"ctx": z * 2 + p // 8, "head": p % 8}

    partner = {"ctx": z * 2 + (1 - ylo)}
    sibling = {"dp": 1 - core}

    def remote(src, dst, s, r, to):
        return pltpu.make_async_remote_copy(
            src_ref=src, dst_ref=dst, send_sem=s, recv_sem=r, device_id=to, device_id_type=MESH
        )

    def wait_for(ref, sem):
        pltpu.make_async_copy(ref, ref, sem).wait()

    key_head = pl.multiple_of((head // KV_GROUP) * HEAD_DIM, HEAD_DIM)
    loads = [
        pltpu.make_async_copy(src, dst, in_s.at[i])
        for i, (src, dst) in enumerate(
            (
                (kv_ref.at[:, :, pl.ds(key_head, HEAD_DIM)], kvbuf.at[0, :, ylo]),
                (q_ref, qbuf.at[ylo]),
                (w_ref, wbuf.at[0]),
                (ids_ref, ids),
                (prio_ref, prio),
                (doc_ref, docs),
                (res_ref, res),
                (gain_ref, gain),
            )
        )
    ]
    for copy in loads:
        copy.start()

    barrier = pltpu.get_barrier_semaphore()

    def greet_plane(j, c):
        pl.semaphore_signal(barrier, inc=1, device_id=at_plane((me + j) % PLANE), device_id_type=MESH)
        return c

    def greet_z(j, c):
        pl.semaphore_signal(barrier, inc=1, device_id=at_z(j), device_id_type=MESH)
        return c

    lax.fori_loop(1, PLANE, greet_plane, 0)
    lax.fori_loop(1, NZ, greet_z, 0)
    pl.semaphore_signal(barrier, inc=1, device_id=sibling, device_id_type=MESH)

    def make_slots():
        row16 = lax.broadcasted_iota(jnp.int32, (16, 128), 0)
        lane16 = lax.broadcasted_iota(jnp.int32, (16, 128), 1)
        expert = lax.broadcasted_iota(jnp.int32, (128, 16), 0)
        chosen = jnp.zeros((128, 16), jnp.float32)
        for k in range(TOPK):
            chosen = chosen + jnp.where(ids[k : k + 1, :] == expert, 1.0, 0.0)
        prio_row = jnp.zeros((16, 128), jnp.int32)
        prio_col = jnp.zeros((16, 128), jnp.int32)
        for u in range(16):
            prio_row = jnp.where(lane16 == u, prio[u], prio_row)
            prio_col = jnp.where(row16 == u, prio[u], prio_col)
        earlier = jnp.where(prio_col < prio_row, 1.0, 0.0)[:, :16]
        ranks = jnp.dot(
            chosen.astype(jnp.bfloat16), earlier.astype(jnp.bfloat16), preferred_element_type=jnp.float32
        )
        slots = jnp.where(chosen > 0.5, ranks + 1.0, 0.0)
        place = jnp.where(lane16 == row16 + 16 * z, 1.0, 0.0)
        mt[...] = jnp.dot(
            slots.astype(jnp.bfloat16), place.astype(jnp.bfloat16), preferred_element_type=jnp.float32
        )

    pl.semaphore_wait(barrier, PLANE - 1 + NZ - 1 + 1)

    def kv_up(r):
        return remote(kvbuf.at[r - 1, :, ylo], kvbuf.at[r, :, ylo], kvu_s.at[r], kvu_r.at[r], at_z(1))

    def kv_side(r):
        return remote(kvbuf.at[r, :, ylo], kvbuf.at[r, :, ylo], kvy_s.at[r], kvy_r.at[r], partner)

    def w_rows(c):
        return pl.ds(pl.multiple_of(core * 512 + c * WROWS, WROWS), WROWS)

    def w_ring(s, c):
        src = w_ref.at[w_rows(c), :] if s in (1, 4) else wbuf.at[s - 1, w_rows(c), :]
        to = at_z(1 if s < 4 else -1)
        return remote(src, wbuf.at[s, w_rows(c), :], w_s.at[s, c], w_r.at[s, c], to)

    def w_side(s, c):
        part = wbuf.at[s, w_rows(c), :]
        return remote(part, part, ws_s.at[s, c], ws_r.at[s, c], sibling)

    def w_forward(s):
        for c in range(WCH):
            w_ring(s, c).wait_recv()
            if s not in (3, 7):
                w_ring(s + 1, c).start()
            w_side(s, c).start()

    q_swap = remote(qbuf.at[ylo], qbuf.at[ylo], q_s, q_r, partner)
    for c in range(WCH):
        w_ring(4, c).start()
    loads[0].wait()
    kv_up(1).start()
    kv_side(0).start()
    loads[1].wait()
    q_swap.start()
    for copy in loads[3:]:
        copy.wait()
    make_slots()

    def mt_copy(j):
        to = (z + j) % NZ
        rows = pl.ds(pl.multiple_of(to * 16, 16), 16)
        return remote(mt.at[rows, :], mtbuf.at[z], mt_s, mt_r, at_z(j))

    def mt_send(j, c):
        mt_copy(j).start()
        return c

    lax.fori_loop(1, NZ, mt_send, 0)
    mtbuf[z] = mt[pl.ds(pl.multiple_of(z * 16, 16), 16), :]

    vt[HEAD_DIM:, :] = jnp.ones((16, 2 * ROWS), jnp.bfloat16)
    row = lax.broadcasted_iota(jnp.int32, (2 * ROWS, ROWS), 0)
    lane = lax.broadcasted_iota(jnp.int32, (1, ROWS), 1)

    def attend(r, yq):
        key_pos = ((z - r + NZ) % NZ) * 256 + row
        pos = (2 * z + yq) * ROWS + lane
        start = jnp.zeros((1, ROWS), jnp.int32)
        end = jnp.int32(0)
        for d in range(DOCS):
            length = docs[d]
            end = end + length
            start = start + jnp.where(pos >= end, length, 0)
        bias = jnp.where((key_pos <= pos) & (key_pos >= start), 0.0, LOW)
        bias = jnp.concatenate([bias, bias], axis=1)
        keys = kvbuf[r, 0].reshape(2 * ROWS, HEAD_DIM)
        vt[:HEAD_DIM, :] = kvbuf[r, 1].reshape(2 * ROWS, HEAD_DIM).T
        for pair in range(HEADS_DEV // 2):
            b = yq * (HEADS_DEV // 2) + pair
            first = pair * 2 * HEAD_DIM
            query = jnp.concatenate(
                [
                    qbuf[yq, :, first : first + HEAD_DIM],
                    qbuf[yq, :, first + HEAD_DIM : first + 2 * HEAD_DIM],
                ],
                axis=0,
            )
            s = lax.dot_general(
                keys, query, (((1,), (1,)), ((), ())), preferred_element_type=jnp.float32
            )
            s = s + bias
            new = jnp.max(s, axis=0, keepdims=True)
            if r > 0:
                old = mx[b]
                new = jnp.maximum(old, new)
            weight = jnp.exp2((s - new) * COEF).astype(jnp.bfloat16)
            out = jnp.dot(vt[...], weight, preferred_element_type=jnp.float32)
            if r > 0:
                out = out + acc[b] * jnp.exp2((old - new) * COEF)
            if r < REACH - 1:
                mx[b] = new
                acc[b] = out
            else:
                mixed = out[:HEAD_DIM] / out[HEAD_DIM : HEAD_DIM + 1]
                rows = pl.ds(pl.multiple_of(yq * ROWS, ROWS), ROWS)
                for i in range(2):
                    one = mixed[:, i * ROWS : (i + 1) * ROWS].T.astype(jnp.bfloat16)
                    att[rows, first + i * HEAD_DIM : first + (i + 1) * HEAD_DIM] = one

    def kv_step(r):
        kv_up(r).wait_recv()
        if r < REACH - 1:
            kv_up(r + 1).start()
        kv_side(r).start()

    kv_step(1)
    kv_side(0).wait_recv()
    attend(0, ylo)
    kv_step(2)
    for c in range(WCH):
        w_ring(1, c).start()
    kv_side(1).wait_recv()
    attend(1, ylo)
    kv_step(3)
    w_forward(4)
    kv_side(2).wait_recv()
    attend(2, ylo)
    kv_step(4)
    q_swap.wait_recv()
    attend(0, 1 - ylo)
    attend(1, 1 - ylo)
    attend(2, 1 - ylo)
    w_forward(1)
    kv_side(3).wait_recv()
    attend(3, ylo)
    attend(3, 1 - ylo)
    w_forward(5)
    kv_side(4).wait_recv()
    attend(4, ylo)
    attend(4, 1 - ylo)

    def p_copy(o, j):
        to = (me + j) % PLANE
        rows = pl.ds(pl.multiple_of(to * 16, 16), 16)
        return remote(psend.at[o, rows, :], prec.at[o, me], p_s.at[o], p_r.at[o], at_plane(to))

    def project(o):
        if o == 0:
            loads[2].wait()
        else:
            for c in range(WCH):
                w_side(o, c).wait_recv()
        part = jnp.dot(att[...], wbuf[o], preferred_element_type=jnp.float32)
        psend[o] = part.astype(jnp.bfloat16)
        prec[o, me] = psend[o, pl.ds(pl.multiple_of(me * 16, 16), 16), :]

        def send(j, c):
            p_copy(o, j).start()
            return c

        lax.fori_loop(1, PLANE, send, 0)

    project(0)
    project(4)
    w_forward(2)
    project(1)
    w_forward(6)
    project(5)
    project(2)
    w_forward(3)
    w_forward(7)
    project(6)
    project(3)
    project(7)

    row16 = lax.broadcasted_iota(jnp.int32, (16, 128), 0)
    lane16 = lax.broadcasted_iota(jnp.int32, (16, 128), 1)
    wait_for(mtbuf.at[pl.ds(0, NZ - 1)], mt_r)
    table = mtbuf[0]
    for i in range(1, NZ):
        table = table + mtbuf[i]
    want = jnp.where(lane16 // 16 == row16 // 2, (row16 % 2 + 1).astype(jnp.float32), -1.0)
    for d in range(PLANE):
        hit = jnp.broadcast_to(table[d : d + 1, :], (16, 128)) == want
        sel[pl.ds(d * 16, 16), :] = jnp.where(hit, 1.0, 0.0).astype(jnp.bfloat16)

    squares = jnp.zeros((16, 1), jnp.float32)
    for o in ORDER:
        wait_for(prec.at[o, pl.ds(0, PLANE - 1)], p_r.at[o])
        for side in range(2):
            total = jnp.zeros((16, 256), jnp.float32)
            for h in range(8):
                total = total + prec[o, side * 8 + h].astype(jnp.float32)
            first = ((z + OFFSET[o] + NZ) % NZ) * 2 + side
            cols = pl.ds(pl.multiple_of(first * 256, 256), 256)
            hidden = (res[:, cols].astype(jnp.float32) + total).astype(jnp.bfloat16)
            hid_ref[:, cols] = hidden
            wide = hidden.astype(jnp.float32)
            squares = squares + jnp.sum(wide * wide, axis=1, keepdims=True)
    inverse = lax.rsqrt(squares / D + 1e-06)

    for g in range(CHUNKS):
        cols = slice(g * CW, (g + 1) * CW)
        normed = hid_ref[:, cols].astype(jnp.float32) * inverse * gain[:, cols]
        xbuf[z, :, cols] = normed.astype(jnp.bfloat16)

    def x_hops(g, way):
        return 4 if g % 2 == way else 3

    def x_ring(g, way, r):
        part = xbuf.at[(z + (1 - r if way == 0 else r - 1) + NZ) % NZ, :, pl.ds(g * CW, CW)]
        return remote(part, part, x_s.at[way, g, r], x_r.at[way, g, r], at_z(1 if way == 0 else -1))

    def a_copy(g, j):
        to = (me + j) % PLANE
        cols = pl.ds(g * CW, CW)
        return remote(
            asend.at[to, :, :, cols], rows_ref.at[:, me, :, cols], a_s.at[g], a_r.at[g], at_plane(to)
        )

    def own_copy(g):
        cols = pl.ds(g * CW, CW)
        return pltpu.make_async_copy(asend.at[me, :, :, cols], rows_ref.at[:, me, :, cols], l_s.at[g])

    for t in range(2 * (CHUNKS - 1) + 5):
        for g in range(CHUNKS):
            r = t - 2 * g
            for way in range(2):
                if 1 <= r <= x_hops(g, way):
                    x_ring(g, way, r).wait_recv()
                if 0 <= r < x_hops(g, way):
                    x_ring(g, way, r + 1).start()
            if r == 4:
                cols = slice(g * CW, (g + 1) * CW)
                gathered = xbuf[:, :, cols].reshape(ROWS, CW)
                picked = jnp.dot(sel[...], gathered, preferred_element_type=jnp.float32)
                asend[:, :, :, cols] = picked.astype(jnp.bfloat16).reshape(PLANE, NZ, 2, CW)

                def send_a(j, c, g=g):
                    a_copy(g, j).start()
                    return c

                lax.fori_loop(1, PLANE, send_a, 0)
                own_copy(g).start()

    for r in range(1, REACH):
        kv_up(r).wait_send()
    for r in range(REACH):
        kv_side(r).wait_send()
    q_swap.wait_send()
    for s in range(1, NZ):
        for c in range(WCH):
            w_ring(s, c).wait_send()
            w_side(s, c).wait_send()
    wait_for(mtbuf.at[pl.ds(0, NZ - 1)], mt_s)
    for o in range(NZ):
        wait_for(prec.at[o, pl.ds(0, PLANE - 1)], p_s.at[o])
    for g in range(CHUNKS):
        for way in range(2):
            for r in range(1, x_hops(g, way) + 1):
                x_ring(g, way, r).wait_send()
        wait_for(asend.at[pl.ds(0, PLANE - 1), :, :, pl.ds(g * CW, CW)], a_s.at[g])
        own_copy(g).wait()
    for g in range(CHUNKS):
        wait_for(asend.at[pl.ds(0, PLANE - 1), :, :, pl.ds(g * CW, CW)], a_r.at[g])


def local(queries, keys_values, doc_lengths, residual, out_weight, norm_gain, expert_ids, priority):
    anywhere = pl.BlockSpec(memory_space=pl.ANY)
    bf16, f32 = jnp.bfloat16, jnp.float32
    dma = pltpu.SemaphoreType.DMA
    hidden, rows = pl.pallas_call(
        kernel,
        out_shape=(
            jax.ShapeDtypeStruct((16, D), bf16),
            jax.ShapeDtypeStruct((NZ, PLANE, 2, D), bf16),
        ),
        in_specs=[anywhere] * 8,
        out_specs=(pl.BlockSpec(memory_space=pltpu.VMEM), anywhere),
        scratch_shapes=[
            pltpu.VMEM((2, ROWS, 1024), bf16),
            pltpu.VMEM((REACH, 2, 2, ROWS, HEAD_DIM), bf16),
            pltpu.VMEM((HEAD_DIM + 16, 2 * ROWS), bf16),
            pltpu.VMEM((HEADS_DEV, 1, 2 * ROWS), f32),
            pltpu.VMEM((HEADS_DEV, HEAD_DIM + 16, 2 * ROWS), f32),
            pltpu.VMEM((2 * ROWS, 1024), bf16),
            pltpu.VMEM((NZ, 1024, 256), bf16),
            pltpu.VMEM((16, D), bf16),
            pltpu.VMEM((1, D), f32),
            pltpu.VMEM((TOPK, 16), jnp.int32),
            pltpu.SMEM((16,), jnp.int32),
            pltpu.SMEM((DOCS,), jnp.int32),
            pltpu.VMEM((128, 128), f32),
            pltpu.VMEM((NZ, 16, 128), f32),
            pltpu.VMEM((256, 128), bf16),
            pltpu.VMEM((NZ, 256, 256), bf16),
            pltpu.VMEM((NZ, PLANE, 16, 256), bf16),
            pltpu.VMEM((NZ, 16, D), bf16),
            pltpu.VMEM((PLANE, NZ, 2, D), bf16),
            dma((8,)),
            dma((REACH,)), dma((REACH,)), dma((REACH,)), dma((REACH,)),
            dma(()), dma(()),
            dma((NZ, WCH)), dma((NZ, WCH)), dma((NZ, WCH)), dma((NZ, WCH)),
            dma(()), dma(()),
            dma((NZ,)), dma((NZ,)),
            dma((2, CHUNKS, 5)), dma((2, CHUNKS, 5)),
            dma((CHUNKS,)), dma((CHUNKS,)), dma((CHUNKS,)),
        ],
        compiler_params=pltpu.CompilerParams(
            collective_id=0, has_side_effects=True, vmem_limit_bytes=60 * 1024 * 1024
        ),
    )(
        queries, keys_values, doc_lengths, residual, out_weight,
        norm_gain.reshape(1, D), expert_ids.T, priority,
    )
    return hidden, rows.reshape(1, PLANE * NZ, 2, D)


def solution(mesh):
    return jax.shard_map(
        local,
        mesh=mesh,
        in_specs=(
            P(("dp", "ctx"), "head"),
            P(None, ("dp", "ctx"), None),
            P("dp"),
            P(("dp", "ctx", "head"), None),
            P("head", "ctx"),
            P(),
            P(("dp", "ctx", "head"), None),
            P(("dp", "ctx", "head")),
        ),
        out_specs=(P(("dp", "ctx", "head"), None), P(("ctx", "head"), "dp", None, None)),
        check_vma=False,
    )
```

time: 126 us -> 101 us (0.80)
  Pallas kernels: 109 us -> 93.5 us
  local copies, waits for them, and re-layouts: 15.5 us -> 6.49 us
    pallas_call x1, Pallas kernels: 109 us -> 93.5 us  [local(): pl.pallas_call(kernel, out_shape=(jax.ShapeDtypeStruct((16, D), bf16), ja...]
    transpose x1 -> x0, local copies, waits for them, and re-layouts: 5.6 us -> none  [local(): rows.reshape(PLANE, NZ, 2, D).transpose(1, 0, 2, 3)]
    reshape x1 -> x0, local copies, waits for them, and re-layouts: 2.63 us -> none  [local(): rows.reshape(PLANE, NZ, 2, D).transpose(1, 0, 2, 3)]
    unnamed x16 -> x2, local copies, waits for them, and re-layouts: 7.28 us -> 6.49 us
where the time goes in v2:
time: 101 us
  Pallas kernels  93.5 us (93%)
  local copies, waits for them, and re-layouts  6.49 us (6%)
    pallas_call x1, Pallas kernels, local(): pl.pallas_call(kernel, out_shape=(jax.ShapeDtypeStruct((16, D), bf16), ja...  93.5 us
    unnamed x2, local copies, waits for them, and re-layouts  6.49 us

profile of v2, /device:TPU:2, one launch (start us, length us, event | category | flops | bytes accessed | tf_op | source)
XLA Modules:
  0.0 100.6 jit_solution(11115831415606721686)
XLA Ops:
  0.6 93.5 %shard_map.95 = (bf16[16,4096]{1,0:T(8,128)(2,1)}, bf16[8,16,2,4096]{3,2,1,0:T(2,128)(2,1)}) custom-call(bf16[128,1024]{1,0:T(8,128)(2,1)} %q_ref.1, bf16[2,128,512]{2,1,0:T(8,128)(2,1)} %kv_ref.1, s32[8]{0:T(128)} %doc_ref.1, bf16[16,4096]{1,0:T(8,128)(2,1)} %res_ref.1, bf16[1024,256]{1,0:T(8,128)(2,1)} %w_ref.1, f32[1,4096]{1,0:T(1,128)} %bitcast.4, ...), custom_call_target="tpu_custom_call" | custom-call | tf_op jit(solution)/shard_map/pallas_call | solution.py:380
  94.2 1.6 %copy.12 = bf16[16,4096]{1,0:T(8,128)(2,1)} copy(bf16[16,4096]{1,0:T(8,128)(2,1)} %get-tuple-element.8) | data formatting | bytes 262144
  95.7 4.9 %copy.13 = bf16[1,128,2,4096]{3,2,1,0:T(2,128)(2,1)} copy(bf16[1,128,2,4096]{3,2,1,0:T(2,128)(2,1)} %bitcast.3) | data formatting | bytes 4194304

commit v3 on v2

v3 whole, which is shorter than its diff:
```python
import math

import jax
import jax.numpy as jnp
from jax import lax
from jax.experimental import pallas as pl
from jax.experimental.pallas import tpu as pltpu
from jax.sharding import PartitionSpec as P

D = 4096
HEAD_DIM = 128
HEADS_DEV = 8
ROWS = 128
KV_GROUP = 2
DOCS = 8
TOPK = 8
NZ = 8
PLANE = 16
REACH = 5
CW = D // NZ
WCH = 4
WROWS = 512 // WCH
LOW = -1e30
COEF = math.log2(math.e) / math.sqrt(HEAD_DIM)
MESH = pl.DeviceIdType.MESH
OFFSET = (0, -1, -2, -3, 1, 2, 3, 4)
SCHEDULE = (
    "k1", "k2", "i1", "v0", "a0", "v1", "a1", "D0", "D1", "v2", "a2", "D2",
    "U0", "D3", "U1", "k3", "k4", "q0", "b0", "D4", "U2", "b1", "D5", "U3",
    "b2", "v3", "a3", "D6", "U4", "v4", "a4", "D7", "U5", "b3", "D8", "U6",
    "b4", "p0", "D9", "U7", "p4", "m0", "D10", "p1", "D11", "U8", "p5", "D12",
    "U9", "p2", "r0", "r4", "D13", "U10", "p6", "D14", "U11", "x0", "x4", "r1",
    "r5", "p3", "D15", "s0", "s4", "p7", "x1", "x5", "r2", "r6", "s1", "s5",
    "x2", "x6", "r3", "r7", "s2", "s6", "x3", "x7", "s3", "s7",
)


def kernel(
    q_ref, kv_ref, doc_ref, res_ref, w_ref, ids_ref, prio_ref,
    hid_out, rows_ref,
    hid_ref, qbuf, kvbuf, vt, mx, acc, att, wbuf, res, ids, prio, docs, mt, mtbuf, sel, psend, prec,
    xbuf, asend,
    in_s, kvu_s, kvu_r, kvy_s, kvy_r, q_s, q_r, w_s, w_r, ws_s, ws_r, mt_s, mt_r,
    p_s, p_r, x_s, x_r, y_s, y_r, a_s, a_r, l_s,
):
    ctx = lax.axis_index("ctx")
    head = lax.axis_index("head")
    core = lax.axis_index("dp")
    z = ctx // 2
    ylo = ctx % 2
    me = ylo * 8 + head

    def at_z(k):
        return {"ctx": ((z + k + NZ) % NZ) * 2 + ylo}

    def at_plane(p):
        return {"ctx": z * 2 + p // 8, "head": p % 8}

    partner = {"ctx": z * 2 + (1 - ylo)}
    sibling = {"dp": 1 - core}
    kind = head % 2
    twin = {"head": head + 1 - 2 * kind}

    def remote(src, dst, s, r, to):
        return pltpu.make_async_remote_copy(
            src_ref=src, dst_ref=dst, send_sem=s, recv_sem=r, device_id=to, device_id_type=MESH
        )

    def wait_for(ref, sem):
        pltpu.make_async_copy(ref, ref, sem).wait()

    key_head = pl.multiple_of((head // KV_GROUP) * HEAD_DIM, HEAD_DIM)
    loads = [
        pltpu.make_async_copy(src, dst, in_s.at[i])
        for i, (src, dst) in enumerate(
            (
                (kv_ref.at[:, :, pl.ds(key_head, HEAD_DIM)], kvbuf.at[0, :, 0]),
                (q_ref, qbuf.at[0]),
                (w_ref, wbuf.at[0]),
                (ids_ref, ids),
                (prio_ref, prio),
                (doc_ref, docs),
                (res_ref, res),
            )
        )
    ]
    for copy in loads:
        copy.start()

    barrier = pltpu.get_barrier_semaphore()

    def greet_plane(j, c):
        pl.semaphore_signal(barrier, inc=1, device_id=at_plane((me + j) % PLANE), device_id_type=MESH)
        return c

    def greet_z(j, c):
        pl.semaphore_signal(barrier, inc=1, device_id=at_z(j), device_id_type=MESH)
        return c

    lax.fori_loop(1, PLANE, greet_plane, 0)
    lax.fori_loop(1, NZ, greet_z, 0)
    pl.semaphore_signal(barrier, inc=1, device_id=sibling, device_id_type=MESH)

    def make_slots():
        row16 = lax.broadcasted_iota(jnp.int32, (16, 128), 0)
        lane16 = lax.broadcasted_iota(jnp.int32, (16, 128), 1)
        expert = lax.broadcasted_iota(jnp.int32, (128, 16), 0)
        chosen = jnp.zeros((128, 16), jnp.float32)
        for k in range(TOPK):
            chosen = chosen + jnp.where(ids[k : k + 1, :] == expert, 1.0, 0.0)
        prio_row = jnp.zeros((16, 128), jnp.int32)
        prio_col = jnp.zeros((16, 128), jnp.int32)
        for u in range(16):
            prio_row = jnp.where(lane16 == u, prio[u], prio_row)
            prio_col = jnp.where(row16 == u, prio[u], prio_col)
        earlier = jnp.where(prio_col < prio_row, 1.0, 0.0)[:, :16]
        ranks = jnp.dot(
            chosen.astype(jnp.bfloat16), earlier.astype(jnp.bfloat16), preferred_element_type=jnp.float32
        )
        slots = jnp.where(chosen > 0.5, ranks + 1.0, 0.0)
        place = jnp.where(lane16 == row16 + 16 * z, 1.0, 0.0)
        mt[...] = jnp.dot(
            slots.astype(jnp.bfloat16), place.astype(jnp.bfloat16), preferred_element_type=jnp.float32
        )

    pl.semaphore_wait(barrier, PLANE - 1 + NZ - 1 + 1)

    def kv_up(r):
        src = kvbuf.at[0 if r < 3 else 2, kind, 0]
        return remote(src, kvbuf.at[r, kind, 0], kvu_s.at[r], kvu_r.at[r], at_z(2 - r % 2))

    def kv_sides(r):
        if r == 0:
            return [remote(kvbuf.at[r, :, 0], kvbuf.at[r, :, 1], kvy_s.at[r, 0], kvy_r.at[r, 0], partner)]
        part = kvbuf.at[r, kind, 0]
        return [
            remote(part, kvbuf.at[r, kind, 1], kvy_s.at[r, 0], kvy_r.at[r, 0], partner),
            remote(part, kvbuf.at[r, kind, 1], kvy_s.at[r, 1], kvy_r.at[r, 1], partner | twin),
            remote(part, part, kvy_s.at[r, 2], kvy_r.at[r, 2], twin),
        ]

    def w_rows(c):
        return pl.ds(pl.multiple_of(core * 512 + c * WROWS, WROWS), WROWS)

    def w_ring(s, c):
        src = w_ref.at[w_rows(c), :] if s in (1, 4) else wbuf.at[s - 1, w_rows(c), :]
        to = at_z(1 if s < 4 else -1)
        return remote(src, wbuf.at[s, w_rows(c), :], w_s.at[s, c], w_r.at[s, c], to)

    def w_side(s, c):
        part = wbuf.at[s, w_rows(c), :]
        return remote(part, part, ws_s.at[s, c], ws_r.at[s, c], sibling)

    def w_forward(first, k):
        s, c = first + k // WCH, k % WCH
        w_ring(s, c).wait_recv()
        if s not in (3, 7):
            w_ring(s + 1, c).start()
        w_side(s, c).start()

    q_swap = remote(qbuf.at[0], qbuf.at[1], q_s, q_r, partner)
    for c in range(WCH):
        w_ring(4, c).start()
    loads[0].wait()
    kv_up(1).start()
    kv_sides(0)[0].start()
    kv_up(2).start()
    loads[1].wait()
    q_swap.start()
    for copy in loads[3:]:
        copy.wait()
    make_slots()

    def mt_copy(j):
        to = (z + j) % NZ
        rows = pl.ds(pl.multiple_of(to * 16, 16), 16)
        return remote(mt.at[rows, :], mtbuf.at[z], mt_s, mt_r, at_z(j))

    def mt_send(j, c):
        mt_copy(j).start()
        return c

    lax.fori_loop(1, NZ, mt_send, 0)
    mtbuf[z] = mt[pl.ds(pl.multiple_of(z * 16, 16), 16), :]

    row = lax.broadcasted_iota(jnp.int32, (2 * ROWS, ROWS), 0)
    lane = lax.broadcasted_iota(jnp.int32, (1, ROWS), 1)

    def attend(r, w):
        yq = ylo if w == 0 else 1 - ylo
        last = r == REACH - 1
        key_pos = ((z - r + NZ) % NZ) * 256 + (row + ylo * ROWS) % 256
        keys = kvbuf[r, 0].reshape(2 * ROWS, HEAD_DIM)
        if w == 0:
            vt[r, :HEAD_DIM, :] = kvbuf[r, 1].reshape(2 * ROWS, HEAD_DIM).T
            vt[r, HEAD_DIM:, :] = jnp.ones((16, 2 * ROWS), jnp.bfloat16)
        pos = (2 * z + yq) * ROWS + lane
        start = jnp.zeros((1, ROWS), jnp.int32)
        end = jnp.int32(0)
        for d in range(DOCS):
            length = docs[d]
            end = end + length
            start = start + jnp.where(pos >= end, length, 0)
        bias = jnp.where((key_pos <= pos) & (key_pos >= start), 0.0, LOW)
        bias = jnp.concatenate([bias, bias], axis=1)
        for pair in range(HEADS_DEV // 2):
            b = w * (HEADS_DEV // 2) + pair
            first = pair * 2 * HEAD_DIM
            query = jnp.concatenate(
                [
                    qbuf[w, :, first : first + HEAD_DIM],
                    qbuf[w, :, first + HEAD_DIM : first + 2 * HEAD_DIM],
                ],
                axis=0,
            )
            s = lax.dot_general(
                keys, query, (((1,), (1,)), ((), ())), preferred_element_type=jnp.float32
            )
            s = s + bias
            new = jnp.max(s, axis=0, keepdims=True)
            if r > 0:
                old = mx[b]
                new = jnp.maximum(old, new)
            weight = jnp.exp2((s - new) * COEF).astype(jnp.bfloat16)
            out = jnp.dot(vt[r], weight, preferred_element_type=jnp.float32)
            if r > 0:
                out = out + acc[b] * jnp.exp2((old - new) * COEF)
            if not last:
                mx[b] = new
                acc[b] = out
            else:
                mixed = out[:HEAD_DIM] / out[HEAD_DIM : HEAD_DIM + 1]
                for i in range(2):
                    one = mixed[:, i * ROWS : (i + 1) * ROWS].T.astype(jnp.bfloat16)
                    att[w, :, first + i * HEAD_DIM : first + (i + 1) * HEAD_DIM] = one

    def kv_step(r):
        kv_up(r).wait_recv()
        if r == 2:
            kv_up(3).start()
            kv_up(4).start()
        for copy in kv_sides(r):
            copy.start()

    def kv_wait(r):
        for copy in kv_sides(r):
            copy.wait_recv()

    def w_begin(s):
        for c in range(WCH):
            w_ring(s, c).start()

    def p_copy(o, w, h):
        to = (ylo if w == 0 else 1 - ylo) * 8 + h
        rows = pl.ds(pl.multiple_of(h * 16, 16), 16)
        return remote(psend.at[o, w, rows, :], prec.at[o, me], p_s.at[o], p_r.at[o], at_plane(to))

    def project(o, sides=(0, 1)):
        if 0 in sides:
            if o == 0:
                loads[2].wait()
            else:
                for c in range(WCH):
                    w_side(o, c).wait_recv()
        count = len(sides) * ROWS
        left = att[...].reshape(count, 1024) if count == 2 * ROWS else att[sides[0]]
        part = jnp.dot(left, wbuf[o], preferred_element_type=jnp.float32).astype(jnp.bfloat16)
        for i, w in enumerate(sides):
            psend[o, w] = part[i * ROWS : (i + 1) * ROWS]
            if w == 0:
                prec[o, me] = psend[o, 0, pl.ds(pl.multiple_of(head * 16, 16), 16), :]

            def send(j, c, w=w):
                p_copy(o, w, (head + j) % 8).start()
                return c

            lax.fori_loop(1 - w, 8, send, 0)

    def make_selection():
        row16 = lax.broadcasted_iota(jnp.int32, (16, 128), 0)
        lane16 = lax.broadcasted_iota(jnp.int32, (16, 128), 1)
        wait_for(mtbuf.at[pl.ds(0, NZ - 1)], mt_r)
        table = mtbuf[0]
        for i in range(1, NZ):
            table = table + mtbuf[i]
        want = jnp.where(lane16 // 16 == row16 // 2, (row16 % 2 + 1).astype(jnp.float32), -1.0)
        for d in range(PLANE):
            hit = jnp.broadcast_to(table[d : d + 1, :], (16, 128)) == want
            sel[pl.ds(d * 16, 16), :] = jnp.where(hit, 1.0, 0.0).astype(jnp.bfloat16)

    def x_copy(o, k, far):
        part = xbuf.at[(z + k + NZ) % NZ, :, pl.ds(o * CW, CW)]
        if k == 0 and far in (2, -2):
            way = 0 if far > 0 else 1
            return remote(part, part, y_s.at[o, way], y_r.at[o, way], at_z(far))
        return remote(part, part, x_s.at[o], x_r.at[o], at_z(far))

    def x_passed(o):
        return ((-2, 1), (2, -1), (-2, 2) if o % 2 else (2, -2))

    def x_forward(o):
        x_copy(o, 0, 2).wait_recv()
        x_copy(o, 0, -2).wait_recv()
        for k, far in x_passed(o):
            x_copy(o, k, far).start()

    def reduce(o):
        wait_for(prec.at[o, pl.ds(0, PLANE - 1)], p_r.at[o])
        halves = []
        for side in range(2):
            total = jnp.zeros((16, 256), jnp.float32)
            for h in range(8):
                total = total + prec[o, side * 8 + h].astype(jnp.float32)
            halves.append(total)
        total = jnp.concatenate(halves, axis=1)
        cols = pl.ds(pl.multiple_of(((z + OFFSET[o] + NZ) % NZ) * CW, CW), CW)
        hidden = (res[:, cols].astype(jnp.float32) + total).astype(jnp.bfloat16)
        hid_ref[:, cols] = hidden
        xbuf[z, :, o * CW : (o + 1) * CW] = hidden

        for far in (2, -2, 1, -1):
            x_copy(o, 0, far).start()

    def a_copy(o, j):
        to = (me + j) % PLANE
        cols = pl.ds(o * CW, CW)
        return remote(asend.at[to, :, cols], rows_ref.at[me, :, cols], a_s.at[o], a_r.at[o], at_plane(to))

    def own_copy(o):
        cols = pl.ds(o * CW, CW)
        return pltpu.make_async_copy(asend.at[me, :, cols], rows_ref.at[me, :, cols], l_s.at[o])

    def select(o):
        wait_for(xbuf.at[pl.ds(0, 5), :, pl.ds(o * CW, CW)], x_r.at[o])
        cols = slice(o * CW, (o + 1) * CW)
        gathered = xbuf[:, :, cols].reshape(ROWS, CW)
        picked = jnp.dot(sel[...], gathered, preferred_element_type=jnp.float32)
        asend[:, :, cols] = picked.astype(jnp.bfloat16).reshape(PLANE, 16, CW)

        def send(j, c):
            a_copy(o, j).start()
            return c

        lax.fori_loop(1, PLANE, send, 0)
        own_copy(o).start()

    hid_copy = pltpu.make_async_copy(hid_ref, hid_out, l_s.at[NZ])

    steps = {
        "a": lambda r: attend(r, 0),
        "b": lambda r: attend(r, 1),
        "k": kv_step,
        "v": kv_wait,
        "q": lambda r: q_swap.wait_recv(),
        "i": w_begin,
        "D": lambda k: w_forward(4, k),
        "U": lambda k: w_forward(1, k),
        "p": project,
        "P": lambda o: project(o, (0,)),
        "Q": lambda o: project(o, (1,)),
        "m": lambda r: make_selection(),
        "r": reduce,
        "x": x_forward,
        "s": select,
    }
    for step in SCHEDULE:
        steps[step[0]](int(step[1:]))
    hid_copy.start()

    hid_copy.wait()
    for r in range(1, REACH):
        kv_up(r).wait_send()
    for r in range(REACH):
        for copy in kv_sides(r):
            copy.wait_send()
    q_swap.wait_send()
    for s in range(1, NZ):
        for c in range(WCH):
            w_ring(s, c).wait_send()
            w_side(s, c).wait_send()
    wait_for(mtbuf.at[pl.ds(0, NZ - 1)], mt_s)
    for o in range(NZ):
        wait_for(prec.at[o, pl.ds(0, PLANE - 1)], p_s.at[o])
        wait_for(xbuf.at[pl.ds(0, 5), :, pl.ds(o * CW, CW)], x_s.at[o])
        for far in (2, -2):
            x_copy(o, 0, far).wait_send()
        wait_for(asend.at[pl.ds(0, PLANE - 1), :, pl.ds(o * CW, CW)], a_s.at[o])
        own_copy(o).wait()
    for o in range(NZ):
        wait_for(asend.at[pl.ds(0, PLANE - 1), :, pl.ds(o * CW, CW)], a_r.at[o])


def finish(
    hid_ref, rows_ref, gain_ref, hid_out, rows_out, hid, rows, gain, wide_gain, out, sem
):
    ins = [pltpu.make_async_copy(gain_ref, gain, sem.at[0, 0]), pltpu.make_async_copy(hid_ref, hid, sem.at[0, 1])]
    for copy in ins:
        copy.start()
    to_hid = pltpu.make_async_copy(hid, hid_out, sem.at[1, 0])

    def row_in(p):
        return pltpu.make_async_copy(rows_ref.at[p], rows.at[p], sem.at[2, p])

    def row_out(p):
        return pltpu.make_async_copy(out.at[:, p], rows_out.at[:, p], sem.at[3, p])

    def begin(p, c):
        row_in(p).start()
        return c

    lax.fori_loop(0, PLANE, begin, 0)
    ins[0].wait()
    for k in range(NZ):
        for o in range(NZ):
            first = ((k + OFFSET[o]) % NZ) * CW
            part = jnp.broadcast_to(gain[:, first : first + CW], (2, CW))
            wide_gain[2 * k : 2 * k + 2, o * CW : (o + 1) * CW] = part
    ins[1].wait()
    to_hid.start()

    def one(p, c):
        row_in(p).wait()
        squares = jnp.zeros((16, CW), jnp.float32)
        for o in range(NZ):
            value = rows[p, :, o * CW : (o + 1) * CW].astype(jnp.float32)
            squares = squares + value * value
        scale = lax.rsqrt(jnp.sum(squares, axis=1, keepdims=True) / D + 1e-06)
        for o in range(NZ):
            cols = slice(o * CW, (o + 1) * CW)
            value = rows[p, :, cols].astype(jnp.float32) * scale * wide_gain[:, cols]
            value = value.astype(jnp.bfloat16).reshape(NZ, 2, CW)
            for k in range(NZ):
                first = ((k + OFFSET[o]) % NZ) * CW
                out[k, p, :, first : first + CW] = value[k]
        row_out(p).start()
        return c

    lax.fori_loop(0, PLANE, one, 0)

    def end(p, c):
        row_out(p).wait()
        return c

    lax.fori_loop(0, PLANE, end, 0)
    to_hid.wait()


def local(queries, keys_values, doc_lengths, residual, out_weight, norm_gain, expert_ids, priority):
    anywhere = pl.BlockSpec(memory_space=pl.ANY)
    bf16, f32 = jnp.bfloat16, jnp.float32
    dma = pltpu.SemaphoreType.DMA
    wide_gain = norm_gain.reshape(1, D)
    hidden, rows = pl.pallas_call(
        kernel,
        out_shape=(
            jax.ShapeDtypeStruct((16, D), bf16),
            jax.ShapeDtypeStruct((PLANE, 16, D), bf16),
        ),
        in_specs=[anywhere] * 7,
        out_specs=(anywhere, anywhere),
        scratch_shapes=[
            pltpu.VMEM((16, D), bf16),
            pltpu.VMEM((2, ROWS, 1024), bf16),
            pltpu.VMEM((REACH, 2, 2, ROWS, HEAD_DIM), bf16),
            pltpu.VMEM((REACH, HEAD_DIM + 16, 2 * ROWS), bf16),
            pltpu.VMEM((HEADS_DEV, 1, 2 * ROWS), f32),
            pltpu.VMEM((HEADS_DEV, HEAD_DIM + 16, 2 * ROWS), f32),
            pltpu.VMEM((2, ROWS, 1024), bf16),
            pltpu.VMEM((NZ, 1024, 256), bf16),
            pltpu.VMEM((16, D), bf16),
            pltpu.VMEM((TOPK, 16), jnp.int32),
            pltpu.SMEM((16,), jnp.int32),
            pltpu.SMEM((DOCS,), jnp.int32),
            pltpu.VMEM((128, 128), f32),
            pltpu.VMEM((NZ, 16, 128), f32),
            pltpu.VMEM((256, 128), bf16),
            pltpu.VMEM((NZ, 2, ROWS, 256), bf16),
            pltpu.VMEM((NZ, PLANE, 16, 256), bf16),
            pltpu.VMEM((NZ, 16, D), bf16),
            pltpu.VMEM((PLANE, 16, D), bf16),
            dma((7,)),
            dma((REACH,)), dma((REACH,)), dma((REACH, 3)), dma((REACH, 3)),
            dma(()), dma(()),
            dma((NZ, WCH)), dma((NZ, WCH)), dma((NZ, WCH)), dma((NZ, WCH)),
            dma(()), dma(()),
            dma((NZ,)), dma((NZ,)),
            dma((NZ,)), dma((NZ,)), dma((NZ, 2)), dma((NZ, 2)),
            dma((NZ,)), dma((NZ,)), dma((NZ + 1,)),
        ],
        compiler_params=pltpu.CompilerParams(
            collective_id=0, has_side_effects=True, vmem_limit_bytes=62 * 1024 * 1024
        ),
    )(
        queries, keys_values, doc_lengths, residual, out_weight,
        expert_ids.T, priority,
    )
    hidden, rows = pl.pallas_call(
        finish,
        out_shape=(
            jax.ShapeDtypeStruct((16, D), bf16),
            jax.ShapeDtypeStruct((NZ, PLANE, 2, D), bf16),
        ),
        in_specs=[anywhere] * 3,
        out_specs=(anywhere, anywhere),
        scratch_shapes=[
            pltpu.VMEM((16, D), bf16),
            pltpu.VMEM((PLANE, 16, D), bf16),
            pltpu.VMEM((1, D), f32),
            pltpu.VMEM((16, D), f32),
            pltpu.VMEM((NZ, PLANE, 2, D), bf16),
            dma((4, PLANE)),
        ],
        compiler_params=pltpu.CompilerParams(vmem_limit_bytes=62 * 1024 * 1024),
    )(hidden, rows, wide_gain)
    return hidden, rows.reshape(1, PLANE * NZ, 2, D)


def solution(mesh):
    return jax.shard_map(
        local,
        mesh=mesh,
        in_specs=(
            P(("dp", "ctx"), "head"),
            P(None, ("dp", "ctx"), None),
            P("dp"),
            P(("dp", "ctx", "head"), None),
            P("head", "ctx"),
            P(),
            P(("dp", "ctx", "head"), None),
            P(("dp", "ctx", "head")),
        ),
        out_specs=(P(("dp", "ctx", "head"), None), P(("ctx", "head"), "dp", None, None)),
        check_vma=False,
    )
```

time: 101 us -> 80.6 us (0.80)
  Pallas kernels: 93.5 us -> 79 us
  local copies, waits for them, and re-layouts: 6.49 us -> 0 us
    pallas_call x1, Pallas kernels: 93.5 us -> 74.4 us  [local(): pl.pallas_call(kernel, out_shape=(jax.ShapeDtypeStruct((16, D), bf16), ja...]
    unnamed x2 -> x0, local copies, waits for them, and re-layouts: 6.49 us -> none
    pallas_call x0 -> x1, Pallas kernels: none -> 4.54 us  [local(): pl.pallas_call(finish, out_shape=(jax.ShapeDtypeStruct((16, D), bf16), ja...]
where the time goes in v3:
time: 80.6 us; the launch traced here: 79.6 us
  Pallas kernels  79 us (98%)
    pallas_call x1, Pallas kernels, local(): pl.pallas_call(kernel, out_shape=(jax.ShapeDtypeStruct((16, D), bf16), ja...  74.4 us
    pallas_call x1, Pallas kernels, local(): pl.pallas_call(finish, out_shape=(jax.ShapeDtypeStruct((16, D), bf16), ja...  4.54 us

profile of v3, /device:TPU:2, one launch (start us, length us, event | category | flops | bytes accessed | tf_op | source)
XLA Modules:
  0.0 79.6 jit_solution(8269278254320899025)
XLA Ops:
  0.6 74.4 %shard_map.95 = (bf16[16,4096]{1,0:T(8,128)(2,1)}, bf16[16,16,4096]{2,1,0:T(8,128)(2,1)}) custom-call(bf16[128,1024]{1,0:T(8,128)(2,1)} %q_ref.1, bf16[2,128,512]{2,1,0:T(8,128)(2,1)} %kv_ref.1, s32[8]{0:T(128)} %doc_ref.1, bf16[16,4096]{1,0:T(8,128)(2,1)} %res_ref.1, bf16[1024,256]{1,0:T(8,128)(2,1)} %w_ref.1, s32[8,16]{1,0:T(8,128)} %bitcast.4, s32[16]{0:T(128)} %prio_ref.1), custom_call_target="tpu_custom_call" | custom-call | tf_op jit(solution)/shard_map/pallas_call | solution.py:453
  75.1 4.5 %shard_map.96 = (bf16[16,4096]{1,0:T(8,128)(2,1)}, bf16[8,16,2,4096]{3,2,1,0:T(2,128)(2,1)}) custom-call(bf16[16,4096]{1,0:T(8,128)(2,1)} %get-tuple-element.6.hid_ref, bf16[16,16,4096]{2,1,0:T(8,128)(2,1)} %get-tuple-element.7.rows_ref, f32[1,4096]{1,0:T(1,128)} %bitcast.3), custom_call_target="tpu_custom_call" | custom-call | tf_op jit(solution)/shard_map/pallas_call | solution.py:497

commit v4 on v3

--- a/solution.py
+++ b/solution.py
@@ -25,13 +25,13 @@
 MESH = pl.DeviceIdType.MESH
 OFFSET = (0, -1, -2, -3, 1, 2, 3, 4)
 SCHEDULE = (
-    "k1", "k2", "i1", "v0", "a0", "v1", "a1", "D0", "D1", "v2", "a2", "D2",
-    "U0", "D3", "U1", "k3", "k4", "q0", "b0", "D4", "U2", "b1", "D5", "U3",
-    "b2", "v3", "a3", "D6", "U4", "v4", "a4", "D7", "U5", "b3", "D8", "U6",
-    "b4", "p0", "D9", "U7", "p4", "m0", "D10", "p1", "D11", "U8", "p5", "D12",
-    "U9", "p2", "r0", "r4", "D13", "U10", "p6", "D14", "U11", "x0", "x4", "r1",
-    "r5", "p3", "D15", "s0", "s4", "p7", "x1", "x5", "r2", "r6", "s1", "s5",
-    "x2", "x6", "r3", "r7", "s2", "s6", "x3", "x7", "s3", "s7",
+    "k1", "i1", "k2", "D0", "v0", "a0", "D1", "v1", "a1", "D2", "v2", "a2",
+    "D3", "U0", "k3", "k4", "D4", "U1", "q0", "b0", "D5", "U2", "b1", "D6",
+    "U3", "v3", "a3", "D7", "U4", "v4", "a4", "D8", "U5", "b2", "D9", "U6",
+    "b3", "D10", "U7", "b4", "p0", "D11", "U8", "p4", "m0", "D12", "U9", "p1",
+    "D13", "U10", "p5", "U11", "p2", "r0", "r4", "U12", "U13", "p6", "r1", "r5",
+    "x0", "x4", "p3", "p7", "x1", "x5", "s0", "s4", "r2", "r6", "s1", "x2",
+    "r3", "s5", "x6", "r7", "s2", "x3", "s6", "x7", "s3", "s7",
 )
 
 
@@ -143,8 +143,10 @@
         return pl.ds(pl.multiple_of(core * 512 + c * WROWS, WROWS), WROWS)
 
     def w_ring(s, c):
-        src = w_ref.at[w_rows(c), :] if s in (1, 4) else wbuf.at[s - 1, w_rows(c), :]
-        to = at_z(1 if s < 4 else -1)
+        up = s < 4 or (s == 7 and c >= WCH // 2)
+        before = 3 if s == 7 and up else s - 1
+        src = w_ref.at[w_rows(c), :] if s in (1, 4) else wbuf.at[before, w_rows(c), :]
+        to = at_z(1 if up else -1)
         return remote(src, wbuf.at[s, w_rows(c), :], w_s.at[s, c], w_r.at[s, c], to)
 
     def w_side(s, c):
@@ -153,8 +155,12 @@
 
     def w_forward(first, k):
         s, c = first + k // WCH, k % WCH
+        if first == 1 and s == 4:
+            s, c = 7, c + WCH // 2
         w_ring(s, c).wait_recv()
-        if s not in (3, 7):
+        if s == 3 and c >= WCH // 2 or s == 6 and c < WCH // 2:
+            w_ring(7, c).start()
+        elif s not in (3, 6, 7):
             w_ring(s + 1, c).start()
         w_side(s, c).start()
 

time: 80.6 us -> 79.4 us (0.985)
  no operation moved by 1% of the time
where the time goes in v4:
time: 79.4 us; the launch traced here: 79.2 us
  Pallas kernels  78.5 us (99%)
    pallas_call x1, Pallas kernels, local(): pl.pallas_call(kernel, out_shape=(jax.ShapeDtypeStruct((16, D), bf16), ja...  74 us
    pallas_call x1, Pallas kernels, local(): pl.pallas_call(finish, out_shape=(jax.ShapeDtypeStruct((16, D), bf16), ja...  4.54 us

profile of v4, /device:TPU:2, one launch (start us, length us, event | category | flops | bytes accessed | tf_op | source)
XLA Modules:
  0.0 79.2 jit_solution(14530039089337839667)
XLA Ops:
  0.6 74.0 %shard_map.95 = (bf16[16,4096]{1,0:T(8,128)(2,1)}, bf16[16,16,4096]{2,1,0:T(8,128)(2,1)}) custom-call(bf16[128,1024]{1,0:T(8,128)(2,1)} %q_ref.1, bf16[2,128,512]{2,1,0:T(8,128)(2,1)} %kv_ref.1, s32[8]{0:T(128)} %doc_ref.1, bf16[16,4096]{1,0:T(8,128)(2,1)} %res_ref.1, bf16[1024,256]{1,0:T(8,128)(2,1)} %w_ref.1, s32[8,16]{1,0:T(8,128)} %bitcast.4, s32[16]{0:T(128)} %prio_ref.1), custom_call_target="tpu_custom_call" | custom-call | tf_op jit(solution)/shard_map/pallas_call | solution.py:459
  74.6 4.5 %shard_map.96 = (bf16[16,4096]{1,0:T(8,128)(2,1)}, bf16[8,16,2,4096]{3,2,1,0:T(2,128)(2,1)}) custom-call(bf16[16,4096]{1,0:T(8,128)(2,1)} %get-tuple-element.6.hid_ref, bf16[16,16,4096]{2,1,0:T(8,128)(2,1)} %get-tuple-element.7.rows_ref, f32[1,4096]{1,0:T(1,128)} %bitcast.3), custom_call_target="tpu_custom_call" | custom-call | tf_op jit(solution)/shard_map/pallas_call | solution.py:503

commit v5 on v4

--- a/solution.py
+++ b/solution.py
@@ -280,7 +280,7 @@
                 p_copy(o, w, (head + j) % 8).start()
                 return c
 
-            lax.fori_loop(1 - w, 8, send, 0)
+            lax.fori_loop(1 - w, 8, send, 0, unroll=True)
 
     def make_selection():
         row16 = lax.broadcasted_iota(jnp.int32, (16, 128), 0)
@@ -347,7 +347,7 @@
             a_copy(o, j).start()
             return c
 
-        lax.fori_loop(1, PLANE, send, 0)
+        lax.fori_loop(1, PLANE, send, 0, unroll=True)
         own_copy(o).start()
 
     hid_copy = pltpu.make_async_copy(hid_ref, hid_out, l_s.at[NZ])

time: 79.4 us -> 79.2 us (level)
  no operation moved by 1% of the time
where the time goes in v5:
time: 79.2 us; the launch traced here: 79 us
  Pallas kernels  78.4 us (99%)
    pallas_call x1, Pallas kernels, local(): pl.pallas_call(kernel, out_shape=(jax.ShapeDtypeStruct((16, D), bf16), ja...  73.9 us
    pallas_call x1, Pallas kernels, local(): pl.pallas_call(finish, out_shape=(jax.ShapeDtypeStruct((16, D), bf16), ja...  4.54 us

profile of v5, /device:TPU:2, one launch (start us, length us, event | category | flops | bytes accessed | tf_op | source)
XLA Modules:
  0.0 79.0 jit_solution(13057063569336147193)
XLA Ops:
  0.6 73.9 %shard_map.95 = (bf16[16,4096]{1,0:T(8,128)(2,1)}, bf16[16,16,4096]{2,1,0:T(8,128)(2,1)}) custom-call(bf16[128,1024]{1,0:T(8,128)(2,1)} %q_ref.1, bf16[2,128,512]{2,1,0:T(8,128)(2,1)} %kv_ref.1, s32[8]{0:T(128)} %doc_ref.1, bf16[16,4096]{1,0:T(8,128)(2,1)} %res_ref.1, bf16[1024,256]{1,0:T(8,128)(2,1)} %w_ref.1, s32[8,16]{1,0:T(8,128)} %bitcast.4, s32[16]{0:T(128)} %prio_ref.1), custom_call_target="tpu_custom_call" | custom-call | tf_op jit(solution)/shard_map/pallas_call | solution.py:459
  74.5 4.5 %shard_map.96 = (bf16[16,4096]{1,0:T(8,128)(2,1)}, bf16[8,16,2,4096]{3,2,1,0:T(2,128)(2,1)}) custom-call(bf16[16,4096]{1,0:T(8,128)(2,1)} %get-tuple-element.6.hid_ref, bf16[16,16,4096]{2,1,0:T(8,128)(2,1)} %get-tuple-element.7.rows_ref, f32[1,4096]{1,0:T(1,128)} %bitcast.3), custom_call_target="tpu_custom_call" | custom-call | tf_op jit(solution)/shard_map/pallas_call | solution.py:503
